TPU v7x, 32 devices: a whole 2x2x4 slice. The times are simulated.
32 devices in a mesh: utt: 4 (over y, core), seq: 8 (over z, x).
Axes of the slice: x: 2, y: 2, z: 4, core: 2. Of those that a mesh axis runs over, the one named last changes fastest.
Arguments:
- inputs: bfloat16 [5632, 1024], P(('utt', 'seq')), may hold values from -6 to 6
- skip_in: bfloat16 [5632, 1024], P(('utt', 'seq')), may hold values from -6 to 6
- lengths: int32 [4, 6], P('utt'), may hold values from 1 to 1320, as said below
- cotangent: bfloat16 [5632, 1024], P(('utt', 'seq')), may hold values from -6 to 6
- w_skip: bfloat16 [2048, 1024], replicated, may hold values from -0.125 to 0.125
- gain_one: float32 [1024], replicated, may hold values from 0.25 to 1.75
- w_qkv: bfloat16 [1024, 3072], replicated, may hold values from -0.1875 to 0.1875
- w_out: bfloat16 [1024, 1024], replicated, may hold values from -3 to 3
- gain_two: float32 [1024], replicated, may hold values from 0.25 to 1.75
- w_up: bfloat16 [1024, 4096], replicated, may hold values from -0.1875 to 0.1875
- b_up: float32 [4096], replicated, may hold values from -3 to 3
- w_down: bfloat16 [4096, 1024], replicated, may hold values from -0.09375 to 0.09375
- b_down: float32 [1024], replicated, may hold values from -3 to 3
Outputs:
- result: bfloat16 [5632, 1024], P(('utt', 'seq'))
- d_inputs: bfloat16 [5632, 1024], P(('utt', 'seq'))
- d_skip: bfloat16 [5632, 1024], P(('utt', 'seq'))
- g_w_skip: float32 [2048, 1024], P('seq')
- g_gain_one: float32 [1024], replicated
- g_w_qkv: float32 [1024, 3072], P('seq')
- g_w_out: float32 [1024, 1024], P('seq')
- g_gain_two: float32 [1024], replicated
- g_w_up: float32 [1024, 4096], P('seq')
- g_b_up: float32 [4096], replicated
- g_w_down: float32 [4096, 1024], P('seq')
- g_b_down: float32 [1024], replicated
Inputs may be any that keep to these rules, and one draw needn't show every extreme that they name: In each group the lengths sum to 1408; exactly one of them, at a slot drawn from the seed, is 1320, and the others sum to 88.
All inputs are finite; a program needn't handle non-finite values.
Results may differ from a plain program's by a relative error of at most 0.02.
Values may be sent and summed in bfloat16 or wider, within the bound.
A program may use at most 192 MiB of HBM per device.

v0:
```python
import functools
import math

import jax
import jax.numpy as jnp
from jax import lax
from jax.experimental import pallas as pl
from jax.experimental.pallas import tpu as pltpu
from jax.sharding import Mesh, PartitionSpec as P

HEAD_DIM = 64
EPSILON = 1e-06
BF = jnp.bfloat16
F32 = jnp.float32
AXES = ("u", "z", "x")
PLANE = ("u", "x")


def dot_nn(a, b):
    return lax.dot_general(a, b, (((1,), (0,)), ((), ())), preferred_element_type=F32)


def dot_nt(a, b):
    return lax.dot_general(a, b, (((1,), (1,)), ((), ())), preferred_element_type=F32)


def dot_tn(a, b):
    return lax.dot_general(a, b, (((0,), (0,)), ((), ())), preferred_element_type=F32)


def attention_forward(q_ref, k_ref, v_ref, col_ref, row_ref, o_ref, lse_ref, acc, out_t):
    forward_heads(q_ref, k_ref, v_ref, col_ref, row_ref[...], o_ref, lse_ref, acc, out_t)


def forward_heads(q_ref, k_ref, v_ref, col_ref, segment_row, o_ref, lse_ref, acc, out_t):
    frames, width = q_ref.shape
    heads = width // HEAD_DIM
    block = frames // (frames // 352)
    lane = lax.broadcasted_iota(jnp.int32, (1, width), 1)
    for h in range(heads):
        own = (lane // HEAD_DIM == h).astype(BF)
        query = q_ref[...] * own
        acc[...] = jnp.zeros_like(acc)

        def step(j, carry):
            top, total = carry
            rows = pl.ds(pl.multiple_of(j * block, block), block)
            scores = dot_nt(k_ref[rows, :], query)
            scores = jnp.where(col_ref[rows, 0:1] == segment_row, scores, -1e30)
            peak = jnp.maximum(top, jnp.max(scores, axis=0, keepdims=True))
            expos = jnp.exp(scores - peak)
            shrink = jnp.exp(top - peak)
            acc[...] = acc[...] * shrink + dot_tn(v_ref[rows, :], expos.astype(BF))
            return peak, total * shrink + jnp.sum(expos, axis=0, keepdims=True)

        top, total = lax.fori_loop(
            0,
            frames // block,
            step,
            (jnp.full((1, frames), -1e30, F32), jnp.zeros((1, frames), F32)),
        )
        part = slice(h * HEAD_DIM, (h + 1) * HEAD_DIM)
        out_t[part, :] = acc[part, :] / total
        lse_ref[h : h + 1, :] = top + jnp.log(total)
    o_ref[...] = out_t[...].T.astype(BF)


def attention_backward(
    q_ref, k_ref, v_ref, o_ref, do_ref, col_ref, row_ref, lse_ref, dq_ref, dk_ref, dv_ref, acc
):
    backward_heads(
        q_ref, k_ref, v_ref, o_ref, do_ref, col_ref, row_ref[...], lse_ref, dq_ref, dk_ref, dv_ref, acc
    )


def backward_heads(
    q_ref, k_ref, v_ref, o_ref, do_ref, col_ref, segment_row, lse_ref, dq_ref, dk_ref, dv_ref, acc
):
    frames, width = q_ref.shape
    heads = width // HEAD_DIM
    block = frames // (frames // 352)
    lane = lax.broadcasted_iota(jnp.int32, (1, width), 1)
    product_t = (o_ref[...].astype(F32) * do_ref[...].astype(F32)).T
    for h in range(heads):
        own = (lane // HEAD_DIM == h).astype(BF)
        query = q_ref[...] * own
        grad = do_ref[...] * own
        part = slice(h * HEAD_DIM, (h + 1) * HEAD_DIM)
        delta = jnp.sum(product_t[part, :], axis=0, keepdims=True)
        log_total = lse_ref[h : h + 1, :]

        def step(j, _):
            rows = pl.ds(pl.multiple_of(j * block, block), block)
            keys = k_ref[rows, :]
            scores = dot_nt(keys, query)
            same = col_ref[rows, 0:1] == segment_row
            probs = jnp.where(same, jnp.exp(scores - log_total), 0.0)
            d_probs = dot_nt(v_ref[rows, :], grad)
            d_scores = (probs * (d_probs - delta)).astype(BF)
            value_part = dot_nn(probs.astype(BF), grad)
            key_part = dot_nn(d_scores, query)
            if h == 0:
                dv_ref[rows, :] = value_part
                dk_ref[rows, :] = key_part
            else:
                dv_ref[rows, :] += value_part
                dk_ref[rows, :] += key_part
            query_part = dot_tn(keys * own, d_scores)

            if h == 0:

                @pl.when(j == 0)
                def _():
                    acc[...] = query_part

                @pl.when(j > 0)
                def _():
                    acc[...] += query_part

            else:
                acc[...] += query_part
            return 0

        lax.fori_loop(0, frames // block, step, 0)
    dq_ref[...] = acc[...].T * (HEAD_DIM**-0.5)


def call_forward(query, keys, values, col, row):
    frames, width = query.shape
    return pl.pallas_call(
        attention_forward,
        out_shape=(
            jax.ShapeDtypeStruct((frames, width), BF),
            jax.ShapeDtypeStruct((width // HEAD_DIM, frames), F32),
        ),
        scratch_shapes=[pltpu.VMEM((width, frames), F32), pltpu.VMEM((width, frames), F32)],
        compiler_params=pltpu.CompilerParams(vmem_limit_bytes=56 * 2**20),
        cost_estimate=pl.CostEstimate(
            flops=16 * frames * frames * width, bytes_accessed=10 * frames * width, transcendentals=0
        ),
        name="attention_forward",
    )(query, keys, values, col, row)


def call_backward(query, keys, values, mixed, grad, col, row, lse):
    frames, width = query.shape
    shape = jax.ShapeDtypeStruct((frames, width), F32)
    return pl.pallas_call(
        attention_backward,
        out_shape=(shape, shape, shape),
        scratch_shapes=[pltpu.VMEM((width, frames), F32)],
        compiler_params=pltpu.CompilerParams(vmem_limit_bytes=56 * 2**20),
        cost_estimate=pl.CostEstimate(
            flops=32 * frames * frames * width, bytes_accessed=20 * frames * width, transcendentals=0
        ),
        name="attention_backward",
    )(query, keys, values, mixed, grad, col, row, lse)


def frame_segments(own_lengths, positions):
    slots = own_lengths.shape[0]
    upto = jnp.arange(slots)[:, None] >= jnp.arange(slots)[None, :]
    ends_at = jnp.sum(jnp.where(upto, own_lengths[None, :], 0), axis=1)
    starts_at = ends_at - own_lengths
    segment = jnp.sum((positions[:, None] >= ends_at[None, :]).astype(jnp.int32), axis=1)
    index = jnp.arange(slots, dtype=jnp.int32)
    offset = jnp.sum(jnp.where(segment[:, None] == index[None, :], starts_at[None, :], 0), axis=1)
    return segment, positions - offset


def rotary_tables(places):
    freqs = jnp.exp(
        jnp.arange(HEAD_DIM // 2, dtype=F32) * (-2.0 * math.log(10000.0) / HEAD_DIM)
    )
    angles = places.astype(F32)[:, None] * freqs[None, :]
    cosine, sine = jnp.cos(angles), jnp.sin(angles)
    return (
        jnp.concatenate([cosine, cosine], axis=1)[:, None, :],
        jnp.concatenate([-sine, sine], axis=1)[:, None, :],
    )


def rotate(v, tables, sign):
    frames, width = v.shape
    shaped = v.reshape(frames, width // HEAD_DIM, HEAD_DIM)
    half = HEAD_DIM // 2
    swapped = jnp.concatenate([shaped[..., half:], shaped[..., :half]], axis=-1)
    return (shaped * tables[0] + swapped * (sign * tables[1])).reshape(frames, width)


def rms_parts(hidden):
    return lax.rsqrt(jnp.mean(hidden * hidden, axis=-1, keepdims=True) + EPSILON)


def rms_back(hidden, inverse, gain, grad):
    scaled = hidden * inverse
    weighted = grad * gain
    inner = jnp.mean(weighted * scaled, axis=-1, keepdims=True)
    return inverse * (weighted - scaled * inner), jnp.sum(grad * scaled, axis=0)


def gelu_both(t):
    bell = 0.5 * (1.0 + lax.erf(t * 0.7071067811865476))
    return t * bell, bell + t * (0.3989422804014327 * jnp.exp(-0.5 * t * t))


TOK = 176
MESH_ID = pl.DeviceIdType.MESH


def flip_low(u):
    return u + 1 - 2 * lax.rem(u, 2)


def flip_high(u):
    return u + 2 - 4 * lax.div(u, 2)


def swap_bits(u):
    return 2 * lax.rem(u, 2) + lax.div(u, 2)


def both(a, b):
    return jnp.logical_and(a, b)


def rms_back_rows(hidden, inverse, gain, grad):
    scaled = hidden * inverse
    weighted = grad * gain
    inner = jnp.mean(weighted * scaled, axis=-1, keepdims=True)
    return inverse * (weighted - scaled * inner), jnp.sum(grad * scaled, axis=0, keepdims=True)


class Sender:
    def __init__(self, send, recv, load):
        self.send, self.recv, self.load = send, recv, load
        self.n = self.m = 0
        self.sent, self.kept = [], []

    def remote(self, src, dst, device, arrival=None):
        copy = pltpu.make_async_remote_copy(
            src_ref=src,
            dst_ref=dst,
            send_sem=self.send.at[self.n],
            recv_sem=self.recv.at[self.n] if arrival is None else arrival,
            device_id=device,
            device_id_type=MESH_ID,
        )
        self.n += 1
        return copy

    def push(self, src, dst, device):
        copy = self.remote(src, dst, device)
        copy.start()
        self.sent.append(copy)
        return copy

    def push_or_keep(self, src, dst, device, own, arrival=None):
        arrival = self.recv.at[self.n] if arrival is None else arrival
        inside = pltpu.make_async_copy(src, dst, arrival)
        copy = self.remote(src, dst, device, arrival)

        @pl.when(own)
        def _():
            inside.start()

        @pl.when(jnp.logical_not(own))
        def _():
            copy.start()

        self.kept.append((copy, own))
        return copy

    def local(self, src, dst):
        copy = pltpu.make_async_copy(src, dst, self.load.at[self.m])
        self.m += 1
        copy.start()
        return copy

    def finish(self):
        for copy in self.sent:
            copy.wait_send()
        for copy, own in self.kept:

            @pl.when(jnp.logical_not(own))
            def _(copy=copy):
                copy.wait_send()

        self.sent, self.kept = [], []


def plane_peers(u, z, x):
    peers = []
    for k in range(8):
        a = flip_low(u) if k & 2 else u
        a = flip_high(a) if k & 4 else a
        b = 1 - x if k & 1 else x
        peers.append(((a, z, b), 2 * a + b))
    return peers


def rows_of(p, start=0, size=TOK):
    return pl.ds(pl.multiple_of(p * TOK + start, 16), size)


class PlaneGather:
    def __init__(self, sender, buffer, peers, start=0, size=TOK):
        self.sender, self.buffer, self.peers = sender, buffer, peers
        self.first, self.size = start, size
        self.low = size // 32 * 16
        self.copies = []

    def pass_on(self, k, to, start=0, size=None):
        rows = rows_of(self.peers[k][1], self.first + start, size or self.size)
        copy = self.sender.remote(self.buffer.at[rows], self.buffer.at[rows], self.peers[to][0])
        copy.start()
        self.copies.append(copy)
        return copy

    def start(self):
        self.x = self.pass_on(0, 1)
        self.y = self.pass_on(0, 4)
        self.cores = [self.pass_on(0, 2)]

    def forward(self):
        self.x.wait_recv()
        self.over_y = self.pass_on(1, 4, self.low, self.size - self.low)
        self.cores.append(self.pass_on(1, 2))
        self.y.wait_recv()
        self.over_x = self.pass_on(4, 1, 0, self.low)
        self.cores.append(self.pass_on(4, 2))

    def corner(self):
        self.over_x.wait_recv()
        self.over_y.wait_recv()
        self.cores.append(self.pass_on(5, 2))

    def core(self, i):
        self.cores[i].wait_recv()

    def left(self):
        for copy in self.copies:
            copy.wait_send()

    def done(self):
        for copy in self.cores:
            copy.wait_recv()
        self.left()


class PlaneSum:
    def __init__(self, sender, terms, first, second, third, place):
        self.sender, self.terms = sender, terms
        self.first, self.second, self.third = first, second, third
        u, z, x = place
        self.low, self.high = lax.rem(z, 2), lax.div(z, 2)
        self.near, self.far = (u, flip_low(z), x), (u, flip_high(z), x)
        self.rows = third.shape[0]
        self.waits = [
            sender.remote(terms.at[self.chunk(j, 1 - self.low)], first.at[j], self.near)
            for j in range(2)
        ]
        sender.sent += self.waits

    def chunk(self, j, low):
        return pl.ds(pl.multiple_of((2 * j + low) * self.rows, self.rows), self.rows)

    def start(self):
        for copy in self.waits:
            copy.start()

    def middle(self):
        for copy in self.waits:
            copy.wait_recv()
        for j in range(2):
            own = self.terms[self.chunk(j, self.low), :].astype(F32)
            self.second[j] = (own + self.first[j].astype(F32)).astype(BF)
        self.wait = self.sender.push(self.second.at[1 - self.high], self.third, self.far)

    def end(self, out):
        self.wait.wait_recv()
        out[...] = (self.second[self.high].astype(F32) + self.third[...].astype(F32)).astype(BF)


class ColumnGather:
    def __init__(self, sender, source, out, peers, x):
        self.sender, self.out, self.peers = sender, out, peers
        rows = out.shape[1]
        me = peers[0][1]

        def part(b):
            return pl.ds(pl.multiple_of(b * rows, rows), rows)

        self.direct = [
            (k, sender.push(source.at[part(peers[k][0][2])], out.at[me], peers[k][0]))
            for k in (5, 4, 1)
        ]
        self.cores = [sender.push(source.at[part(x)], out.at[me], peers[2][0])]
        out[me] = source[part(x), :]

    def forward(self):
        for k, copy in self.direct:
            copy.wait_recv()
            slot = self.out.at[self.peers[k][1]]
            self.cores.append(self.sender.push(slot, slot, self.peers[2][0]))

    def done(self):
        for copy in self.cores:
            copy.wait_recv()


class RowGather:
    def __init__(self, sender, source, out, peers, u):
        self.sender, self.out, self.peers = sender, out, peers
        self.rows = source.shape[0]
        self.far = sender.push(source, out.at[self.part(u)], peers[4][0])
        self.cores = [sender.push(source, out.at[self.part(u)], peers[2][0])]
        out[self.part(u), :] = source[...]

    def part(self, u):
        return pl.ds(pl.multiple_of(u * self.rows, self.rows), self.rows)

    def forward(self):
        self.far.wait_recv()
        block = self.out.at[self.part(self.peers[4][0][0])]
        self.cores.append(self.sender.push(block, block, self.peers[2][0]))

    def done(self):
        for copy in self.cores:
            copy.wait_recv()


def layer_kernel(
    lengths_ref,
    gain_one_ref,
    gain_two_ref,
    b_up_ref,
    b_down_ref,
    inputs_ref,
    skip_ref,
    cot_ref,
    w_skip_ref,
    w_qkv_ref,
    w_out_ref,
    w_up_ref,
    w_down_ref,
    result_out,
    inputs_out,
    skip_out,
    g_skip_out,
    g_qkv_out,
    g_out_out,
    g_up_out,
    g_down_out,
    vector_out,
    normed_kept,
    wide_a,
    wide_b,
    w_out,
    n2,
    ct,
    db,
    joined,
    q,
    k,
    v,
    o,
    grad,
    lse,
    cos_t,
    sin_t,
    seg,
    entry,
    middle,
    down_sum,
    normed_sum,
    result,
    result_r,
    d_mixed,
    d_heads,
    d_frames,
    entry_r,
    gd,
    gu,
    gq,
    gs,
    go,
    d1,
    d2,
    d3,
    dz,
    u1,
    u2,
    u3,
    uz,
    q1,
    q2,
    q3,
    qz,
    s1,
    s2,
    s3,
    sz,
    o1,
    o2,
    fin_d,
    fin_u,
    fin_q,
    fin_s,
    fin_o,
    vec,
    vec_plane,
    vec_sum,
    vec_z,
    acc,
    lens,
    lens_r,
    send,
    recv,
    load,
    spread,
):
    u, z, x = (lax.axis_index(a) for a in AXES)
    me = 2 * u + x
    peers = plane_peers(u, z, x)
    place = (u, z, x)
    d = entry.shape[1]
    group = n2.shape[0]
    hidden = wide_a.shape[1]
    heads_at = pl.ds(pl.multiple_of(me * 128, 128), 128)
    plane = swap_bits(u)
    away = (z, plane, x)
    stays_away = both(u == z, plane == z)
    own_home = swap_bits(z)
    home = (own_home, u, x)
    stays_home = both(own_home == u, u == z)
    sender = Sender(send, recv, load)
    mine = rows_of(me)
    low, high = 80, 96

    got_x = sender.local(inputs_ref, gd.at[pl.ds(0, TOK)])
    got_s = sender.local(skip_ref, gd.at[pl.ds(TOK, TOK)])
    got_w = [
        sender.local(w_skip_ref.at[pl.ds(i * d, d)], wide_b.at[pl.ds(i * d, d)]) for i in range(2)
    ]
    got_q = [
        sender.local(
            w_qkv_ref.at[:, pl.ds(pl.multiple_of(c * d + me * 128, 128), 128)],
            wide_a.at[:, pl.ds(c * 128, 128)],
        )
        for c in range(3)
    ]
    slots = lengths_ref.shape[1]
    for s in range(slots):
        lens[s : s + 1, :] = jnp.full((1, 128), lengths_ref[0, s].astype(F32), F32)
    lens[slots:8, :] = jnp.zeros((8 - slots, 128), F32)
    sent_lens = sender.push_or_keep(lens, lens_r, away, stays_away)
    got_x.wait()
    got_w[0].wait()
    value = dot_nn(gd[:TOK, :], wide_b[:d, :])
    got_s.wait()
    got_w[1].wait()
    d_mixed[...] = (value + dot_nn(gd[TOK : 2 * TOK, :], wide_b[d : 2 * d, :])).astype(BF)
    sent_entry = [
        sender.push_or_keep(
            d_mixed.at[pl.ds(a, n)], entry.at[pl.ds(a, n)], away, stays_away
        )
        for a, n in ((0, low), (low, high))
    ]
    got_down = sender.local(w_down_ref, wide_b)
    got_out = sender.local(w_out_ref, w_out)

    def joined_block(j):
        return slice(j // 2 * TOK, (j // 2 + 1) * TOK), slice(j % 2 * 256, (j % 2 + 1) * 256)

    lane = lax.broadcasted_iota(jnp.int32, (TOK, 128), 1)
    for a in range(4):
        for b in range(2):
            for pair in range(2):
                halves = []
                for s in range(2):
                    block = 4 * (2 * pair + s) + 2 * b + a // 2
                    top = block // (d // 128) * TOK
                    first = block % (d // 128) * 128
                    piece = gd[top : top + TOK, first : first + 128].astype(F32)
                    if a % 2 != s:
                        piece = pltpu.roll(piece, 64, 1)
                    halves.append(piece)
                j = 2 * a + b
                gu[
                    j // 2 * TOK : (j // 2 + 1) * TOK,
                    j % 2 * 256 + pair * 128 : j % 2 * 256 + (pair + 1) * 128,
                ] = jnp.where(lane < 64, halves[0], halves[1]).astype(BF)

    sent_lens.wait_recv()
    freqs = jnp.exp(lax.rem(lane, 32).astype(F32) * (-2.0 * math.log(10000.0) / HEAD_DIM))
    front = lax.rem(lane, 64) < 32
    sign = jnp.where(front, -1.0, 1.0)

    def table(i, _):
        rows = rows_of(i)
        at = (lax.broadcasted_iota(jnp.int32, (TOK, 128), 0) + i * TOK).astype(F32)
        spot, segment, end = at, jnp.zeros_like(at), jnp.zeros((1, 128), F32)
        for s in range(slots):
            length = lens_r[s : s + 1, :]
            end = end + length
            past = at >= end
            segment = segment + jnp.where(past, 1.0, 0.0)
            spot = spot - jnp.where(past, length, 0.0)
        angle = spot * freqs
        cos_t[rows, :] = jnp.cos(angle)
        sin_t[rows, :] = jnp.sin(angle) * sign
        seg[rows, :] = segment
        return 0

    lax.fori_loop(0, group // TOK, table, 0)
    at = lax.broadcasted_iota(jnp.int32, (1, group), 1).astype(F32)
    segment_row, end = jnp.zeros((1, group), F32), jnp.zeros((1, 1), F32)
    for s in range(slots):
        end = end + lens_r[s : s + 1, 0:1]
        segment_row = segment_row + jnp.where(at >= end, 1.0, 0.0)
    lse[2:3, :] = segment_row
    for copy in got_q:
        copy.wait()

    def turn(t, rows, way):
        swapped = jnp.where(front, pltpu.roll(t, 96, 1), pltpu.roll(t, 32, 1))
        return t * cos_t[rows, :] + swapped * (way * sin_t[rows, :])

    def project(i):
        rows = rows_of(peers[i][1])
        value = dot_nn(n2[rows, :], wide_a[:, :384])
        q[rows, :] = (
            turn(value[:, :128], rows, 1.0).astype(BF).astype(F32) * HEAD_DIM**-0.5
        ).astype(BF)
        k[rows, :] = turn(value[:, 128:256], rows, 1.0).astype(BF)
        v[rows, :] = value[:, 256:].astype(BF)

    first_a = PlaneGather(sender, n2, peers, 0, low)
    first_b = PlaneGather(sender, n2, peers, low, high)
    for copy, gather, (a, n) in zip(sent_entry, (first_a, first_b), ((0, low), (low, high))):
        copy.wait_recv()
        value = entry[a : a + n, :].astype(F32)
        n2[rows_of(me, a, n), :] = (value * rms_parts(value) * gain_one_ref[...]).astype(BF)
        gather.start()
    sent_cot = sender.push_or_keep(cot_ref, ct.at[rows_of(2 * z + x)], away, stays_away)
    first_a.forward()
    project(0)
    first_a.core(0)
    first_b.core(0)
    project(2)
    first_b.forward()
    project(1)
    project(4)
    first_a.corner()
    first_b.corner()
    project(5)
    for gather in (first_a, first_b):
        gather.core(1)
    project(3)
    for gather in (first_a, first_b):
        gather.core(2)
    project(6)
    for gather in (first_a, first_b):
        gather.core(3)
    project(7)
    got_up = sender.local(w_up_ref, wide_a)
    kept_normed = sender.local(n2, normed_kept)
    sent_cot.wait_recv()
    gather_cot = PlaneGather(sender, ct, peers)
    gather_cot.start()
    for a in range(4):
        for b in range(2):
            rows, cols = joined_block(2 * a + b)
            sender.push_or_keep(
                gu.at[rows, cols],
                joined.at[rows_of(2 * z + x)],
                (a, plane, b),
                both(both(u == a, x == b), plane == z),
                spread.at[2 * z + x],
            )

    pl.run_scoped(
        lambda out_t: forward_heads(q, k, v, seg, segment_row, o, lse, acc, out_t),
        pltpu.VMEM((128, group), F32),
    )
    kept_normed.wait()
    for gather in (first_a, first_b):
        gather.left()
    own_mixed = sender.local(o.at[mine], d_frames.at[0, :, heads_at])
    got_mixed = [
        sender.push(o.at[rows_of(peers[i][1])], d_frames.at[0, :, heads_at], peers[i][0])
        for i in range(1, 8)
    ]
    gather_cot.forward()
    own_mixed.wait()
    for copy in got_mixed:
        copy.wait_recv()

    got_out.wait()
    value = entry[...].astype(F32) + dot_nn(d_frames[0], w_out[...])
    middle[...] = value
    n2[mine, :] = (value * rms_parts(value) * gain_two_ref[...]).astype(BF)
    gather_normed = PlaneGather(sender, n2, peers)
    gather_normed.start()

    down_sum[...] = jnp.zeros_like(down_sum)
    normed_sum[...] = jnp.zeros_like(normed_sum)
    got_up.wait()
    got_down.wait()
    step = 512

    def feed(c, _):
        cols = pl.ds(pl.multiple_of(c * step, step), step)
        up = dot_nn(n2[mine, :], wide_a[:, cols]) + b_up_ref[:, cols]
        active, slope = gelu_both(up)
        d_up = (dot_nt(ct[mine, :], wide_b[cols, :]) * slope).astype(BF)
        down_sum[...] += dot_nn(active.astype(BF), wide_b[cols, :])
        normed_sum[...] += dot_nt(d_up, wide_a[:, cols])
        vec[pl.ds(8 + c, 1), :] = jnp.sum(d_up.astype(F32), axis=0, keepdims=True)
        return 0

    half = hidden // step // 2
    lax.fori_loop(0, half, feed, 0)
    gather_cot.corner()
    lax.fori_loop(half, 2 * half, feed, 0)
    gather_normed.forward()
    value = middle[...]
    inverse = rms_parts(value)
    back, g_gain_two = rms_back_rows(value, inverse, gain_two_ref[...], normed_sum[...])
    grad_out = ct[mine, :].astype(F32)
    d_middle = grad_out + back
    result[...] = (value + down_sum[...] + b_down_ref[...]).astype(BF)
    middle[...] = d_middle
    db[mine, :] = d_middle.astype(BF)
    for copy, own in sender.kept[1:3]:

        @pl.when(jnp.logical_not(own))
        def _(copy=copy):
            copy.wait_send()

    sender.kept = sender.kept[:1] + sender.kept[3:]
    d_mixed[...] = dot_nt(db[mine, :], w_out[...]).astype(BF)
    own_grad = sender.local(d_mixed.at[:, heads_at], grad.at[mine])
    got_grad = [
        sender.push(
            d_mixed.at[:, pl.ds(pl.multiple_of(peers[i][1] * 128, 128), 128)],
            grad.at[mine],
            peers[i][0],
        )
        for i in range(1, 8)
    ]
    sent_result = sender.push_or_keep(result, result_r, home, stays_home)
    g_b_down = jnp.sum(grad_out, axis=0, keepdims=True)
    for i in range(2):
        part = slice(i * d // 2, (i + 1) * d // 2)
        vec[2 + i : 3 + i, :] = g_gain_two[:, part]
        vec[4 + i : 5 + i, :] = g_b_down[:, part]
    vec[6:8, :] = jnp.zeros((2, step), F32)
    gather_cot.done()
    gather_normed.corner()
    gather_branch = PlaneGather(sender, db, peers)
    gather_branch.start()
    gather_normed.done()
    for j in range(8):
        rows, cols = joined_block(j)
        copy, own = sender.kept[2 + j]

        @pl.when(jnp.logical_not(own))
        def _(copy=copy):
            copy.wait_send()

    sender.kept = sender.kept[:2] + sender.kept[10:]
    for s in range(8):
        rows = pl.ds(s * TOK, TOK)
        pltpu.make_async_copy(joined.at[rows], joined.at[rows], spread.at[s]).wait()

    chunk = hidden // 32
    sum_down = PlaneSum(sender, gd, d1, d2, d3, place)
    sum_up = PlaneSum(sender, gu, u1, u2, u3, place)

    def own_units(w_up_own, w_down_own, active, d_up):
        copies, starts = [], []
        for s in range(4):
            first = pl.multiple_of((2 * s + x) * (4 * chunk) + u * chunk, chunk)
            starts.append(first)
            copies.append(
                sender.local(
                    w_up_ref.at[:, pl.ds(first, chunk)], w_up_own.at[:, pl.ds(s * chunk, chunk)]
                )
            )
            copies.append(
                sender.local(
                    w_down_ref.at[pl.ds(first, chunk)], w_down_own.at[pl.ds(s * chunk, chunk)]
                )
            )
        for copy in copies:
            copy.wait()
        bias = jnp.concatenate([b_up_ref[:, pl.ds(first, chunk)] for first in starts], axis=1)

        def units(i, _):
            rows = rows_of(i)
            up = dot_nn(n2[rows, :], w_up_own[...]) + bias
            act, slope = gelu_both(up)
            active[rows, :] = act.astype(BF)
            d_up[rows, :] = (dot_nt(ct[rows, :], w_down_own[...]) * slope).astype(BF)
            return 0

        lax.fori_loop(0, group // TOK, units, 0)

        def down_terms(i, _):
            cols = pl.ds(pl.multiple_of(i * 256, 256), 256)
            gd[cols, :] = dot_tn(active[:, cols], ct[...]).astype(BF)
            return 0

        lax.fori_loop(0, 4 * chunk // 256, down_terms, 0)
        sum_down.start()

        def up_terms(i, _):
            cols = pl.ds(pl.multiple_of(i * 256, 256), 256)
            gu[cols, :] = dot_tn(n2[:, cols], d_up[...]).astype(BF)
            return 0

        lax.fori_loop(0, d // 256, up_terms, 0)
        sum_up.start()

    pl.run_scoped(
        own_units,
        pltpu.VMEM((d, 4 * chunk), BF),
        pltpu.VMEM((4 * chunk, d), BF),
        pltpu.VMEM((group, 4 * chunk), BF),
        pltpu.VMEM((group, 4 * chunk), BF),
    )
    got_normed = sender.local(normed_kept, ct)
    got_qkv = sender.local(w_qkv_ref, wide_a.at[:, pl.ds(0, 3 * d)])
    got_skip = sender.local(w_skip_ref, wide_b.at[pl.ds(0, 2 * d)])
    gather_branch.forward()
    own_grad.wait()
    for copy in got_grad:
        copy.wait_recv()

    def heads(dq, dk, dv):
        backward_heads(q, k, v, o, grad, seg, lse[2:3, :], lse, dq, dk, dv, acc)

        def turn_back(i, _):
            rows = rows_of(i)
            for c, ref in ((0, dq), (1, dk)):
                t = ref[rows, :].astype(BF).astype(F32)
                d_heads[c, rows, :] = turn(t, rows, -1.0).astype(BF)
            d_heads[2, rows, :] = dv[rows, :].astype(BF)
            return 0

        lax.fori_loop(0, group // TOK, turn_back, 0)

    pl.run_scoped(heads, *[pltpu.VMEM((group, 128), F32)] * 3)
    own_frames = sender.local(d_heads.at[:, mine], d_frames.at[:, :, heads_at])
    got_frames = [
        sender.push(
            d_heads.at[:, rows_of(peers[i][1])], d_frames.at[:, :, heads_at], peers[i][0]
        )
        for i in range(1, 8)
    ]
    gather_branch.corner()
    got_normed.wait()

    def qkv_terms(i, _):
        cols = pl.ds(pl.multiple_of(i * 256, 256), 256)
        turned = ct[:, cols].T
        for c in range(3):
            gq[cols, c * 128 : (c + 1) * 128] = dot_nn(turned, d_heads[c]).astype(BF)
        return 0

    lax.fori_loop(0, d // 256, qkv_terms, 0)
    sum_qkv = PlaneSum(sender, gq, q1, q2, q3, place)
    sum_qkv.start()
    gather_branch.done()
    go[...] = dot_tn(o[...], db[...]).astype(BF)

    same_high = lax.div(z, 2) == lax.div(u, 2)
    same_low = lax.rem(z, 2) == lax.rem(u, 2)
    owner = z == u
    to_far = sender.remote(go, o1, (u, flip_high(z), x))
    to_near = sender.remote(go, o2, (u, flip_low(z), x))

    @pl.when(jnp.logical_not(same_high))
    def _():
        to_far.start()

    sum_down.middle()
    sum_up.middle()

    own_frames.wait()
    for copy in got_frames:
        copy.wait_recv()
    got_qkv.wait()
    d_normed = dot_nt(d_frames[0], wide_a[:, :d])
    d_normed += dot_nt(d_frames[1], wide_a[:, d : 2 * d])
    d_normed += dot_nt(d_frames[2], wide_a[:, 2 * d : 3 * d])
    value = entry[...].astype(F32)
    back, g_gain_one = rms_back_rows(value, rms_parts(value), gain_one_ref[...], d_normed)
    n2[mine, :] = (middle[...] + back).astype(BF)
    gather_entry = PlaneGather(sender, n2, peers)
    gather_entry.start()
    sent_back = sender.push_or_keep(n2.at[mine], entry_r, home, stays_home)

    for i in range(2):
        vec[i : i + 1, :] = g_gain_one[:, i * d // 2 : (i + 1) * d // 2]
    vec_at = pl.ds(pl.multiple_of(me * 16, 16), 16)
    got_vec = [sender.push(vec, vec_plane.at[vec_at], peers[i][0]) for i in range(1, 8)]
    vec_plane[vec_at, :] = vec[...]

    def skip_terms(i):
        rows = rows_of(peers[i][1])
        return dot_tn(joined[rows, :], n2[rows, :])

    total = skip_terms(0)

    @pl.when(same_high)
    def _():
        to_far.wait_recv()
        go[...] = (go[...].astype(F32) + o1[...].astype(F32)).astype(BF)

    @pl.when(both(same_high, jnp.logical_not(same_low)))
    def _():
        to_near.start()

    gather_entry.forward()
    total += skip_terms(1)
    total += skip_terms(4)
    gather_entry.corner()
    total += skip_terms(5)
    for copy in gather_entry.cores:
        copy.wait_recv()
    for i in (2, 3, 6, 7):
        total += skip_terms(i)
    gs[...] = total.astype(BF)
    sum_skip = PlaneSum(sender, gs, s1, s2, s3, place)
    sum_skip.start()

    sum_qkv.middle()
    for copy in got_vec:
        copy.wait_recv()
    value = vec_plane[0:16, :]
    for i in range(1, 8):
        value += vec_plane[16 * i : 16 * (i + 1), :]
    vec_sum[...] = value
    z_devices = (
        (u, flip_low(z), x),
        (u, flip_high(z), x),
        (u, flip_low(flip_high(z)), x),
    )
    vec_at = pl.ds(pl.multiple_of(z * 16, 16), 16)
    got_vec = [sender.push(vec_sum, vec_z.at[vec_at], device) for device in z_devices]
    vec_z[vec_at, :] = vec_sum[...]

    sum_up.end(uz)
    last_up = ColumnGather(sender, uz, fin_u, peers, x)
    sum_down.end(dz)
    last_down = RowGather(sender, dz, fin_d, peers, u)

    sum_skip.middle()

    outs = []
    sent_back.wait_recv()
    got_skip.wait()
    for i, out in enumerate((inputs_out, skip_out)):
        d_frames[i] = dot_nt(entry_r[...], wide_b[i * d : (i + 1) * d, :]).astype(BF)
        outs.append(sender.local(d_frames.at[i], out))
    sum_qkv.end(qz)
    last_qkv = ColumnGather(sender, qz, fin_q, peers, x)

    @pl.when(owner)
    def _():
        to_near.wait_recv()
        fin_o[...] = (go[...].astype(F32) + o2[...].astype(F32)).astype(BF)

    def tell(i, to):
        return pltpu.make_async_remote_copy(
            src_ref=fin_o,
            dst_ref=fin_o,
            send_sem=spread.at[8 + i],
            recv_sem=spread.at[11],
            device_id=peers[to][0],
            device_id_type=MESH_ID,
        )

    tell_core, tell_far, tell_on = tell(0, 2), tell(1, 4), tell(2, 2)

    @pl.when(owner)
    def _():
        tell_far.start()
        tell_core.start()

    last_up.forward()
    last_down.forward()
    sum_skip.end(sz)
    last_skip = RowGather(sender, sz, fin_s, peers, u)
    last_qkv.forward()
    across = u == flip_high(z)

    @pl.when(jnp.logical_not(owner))
    def _():
        tell_core.wait_recv()

    @pl.when(across)
    def _():
        tell_on.start()

    last_up.done()
    for p in range(8):
        for s in range(4):
            first = (2 * s + p % 2) * 4 * chunk + p // 2 * chunk
            outs.append(
                sender.local(
                    fin_u.at[p, :, pl.ds(s * chunk, chunk)], g_up_out.at[:, pl.ds(first, chunk)]
                )
            )
    last_down.done()
    outs.append(sender.local(fin_d, g_down_out))
    for copy in got_vec:
        copy.wait_recv()
    vec_sum_out = vec_z[0:16, :] + vec_z[16:32, :] + vec_z[32:48, :] + vec_z[48:64, :]
    vec_plane[0:16, :] = vec_sum_out
    outs.append(sender.local(vec_plane.at[pl.ds(0, 16)], vector_out))
    sent_result.wait_recv()
    outs.append(sender.local(result_r, result_out))
    outs.append(sender.local(fin_o, g_out_out))
    last_skip.forward()
    last_qkv.done()
    for p in range(8):
        for c in range(3):
            outs.append(
                sender.local(
                    fin_q.at[p, :, pl.ds(c * 128, 128)],
                    g_qkv_out.at[:, pl.ds(c * d + p * 128, 128)],
                )
            )

    @pl.when(owner)
    def _():
        tell_far.wait_send()
        tell_core.wait_send()

    @pl.when(across)
    def _():
        tell_on.wait_send()

    @pl.when(jnp.logical_not(same_high))
    def _():
        to_far.wait_send()

    @pl.when(both(same_high, jnp.logical_not(same_low)))
    def _():
        to_near.wait_send()

    last_skip.done()
    outs.append(sender.local(fin_s, g_skip_out))
    for copy in outs:
        copy.wait()
    gather_entry.left()
    sender.finish()


def call_layer(arrays, lengths, vectors):
    d = arrays[0].shape[1]
    hidden = arrays[6].shape[1]
    group = 8 * TOK
    any_space = pl.BlockSpec(memory_space=pl.ANY)
    vmem = pl.BlockSpec(memory_space=pltpu.VMEM)
    smem = pl.BlockSpec(memory_space=pltpu.SMEM)
    block, wide = ((TOK, d), BF), ((group, d), BF)
    head, table, total = ((group, 128), BF), ((group, 128), F32), ((TOK, d), F32)
    unit = hidden // 8

    def sums(rows, columns):
        return [
            ((2, rows, columns), BF),
            ((2, rows, columns), BF),
            ((rows, columns), BF),
            ((rows, columns), BF),
        ]

    outs = [
        block,
        block,
        block,
        ((2 * d // 8, d), BF),
        ((d // 8, 3 * d), BF),
        ((d // 8, d), BF),
        ((d // 8, hidden), BF),
        ((unit, d), BF),
        ((16, 512), F32),
        wide,
    ]
    scratch = [
        ((d, hidden), BF),
        ((hidden, d), BF),
        ((d, d), BF),
        wide,
        wide,
        wide,
        ((group, 256), BF),
        head,
        head,
        head,
        head,
        head,
        ((8, group), F32),
        table,
        table,
        table,
        block,
        total,
        total,
        total,
        block,
        block,
        block,
        ((3, group, 128), BF),
        ((3, TOK, d), BF),
        block,
        ((unit, d), BF),
        ((d, unit), BF),
        ((d, 384), BF),
        ((256, d), BF),
        ((128, d), BF),
        *sums(unit // 4, d),
        *sums(d // 4, unit),
        *sums(d // 4, 384),
        *sums(64, d),
        ((128, d), BF),
        ((128, d), BF),
        ((unit, d), BF),
        ((8, d // 8, unit), BF),
        ((8, d // 8, 384), BF),
        ((256, d), BF),
        ((128, d), BF),
        ((16, 512), F32),
        ((128, 512), F32),
        ((16, 512), F32),
        ((64, 512), F32),
        ((128, group), F32),
        ((8, 128), F32),
        ((8, 128), F32),
    ]
    made = pl.pallas_call(
        layer_kernel,
        in_specs=[smem] + [vmem] * len(vectors) + [any_space] * len(arrays),
        out_specs=[any_space] * len(outs),
        out_shape=[jax.ShapeDtypeStruct(*o) for o in outs],
        scratch_shapes=[pltpu.VMEM(*s) for s in scratch]
        + [pltpu.SemaphoreType.DMA((160,))] * 3
        + [pltpu.SemaphoreType.DMA((12,))],
        compiler_params=pltpu.CompilerParams(
            vmem_limit_bytes=60 * 2**20 + 2**18, has_side_effects=True
        ),
        name="layer",
    )(lengths, *vectors, *arrays)
    return made[:9]


def widen_kernel(*refs):
    n = 9
    ins, outs = refs[:n], refs[n:]
    for i in range(8):
        outs[i][...] = ins[i][...].astype(outs[i].dtype)
    vectors = ins[8]
    for out, row in zip(outs[8:], (0, 2, 4, 8)):
        for part in range(out.shape[1] // 512):
            out[:, part * 512 : (part + 1) * 512] = vectors[row + part : row + part + 1, :]


def call_widen(made):
    steps = 8
    whole = [pl.BlockSpec(a.shape, lambda i: (0, 0)) for a in made]
    parts = [
        pl.BlockSpec((a.shape[0] // steps, a.shape[1]), lambda i: (i, 0)) for a in made[3:8]
    ]
    d, hidden = made[5].shape[1], made[6].shape[1]
    ends = [(1, d), (1, d), (1, d), (1, hidden)]
    outs = pl.pallas_call(
        widen_kernel,
        grid=(steps,),
        in_specs=whole[:3] + parts + whole[8:],
        out_specs=whole[:3] + parts + [pl.BlockSpec(e, lambda i: (0, 0)) for e in ends],
        out_shape=[jax.ShapeDtypeStruct(a.shape, BF) for a in made[:3]]
        + [jax.ShapeDtypeStruct(a.shape, F32) for a in made[3:8]]
        + [jax.ShapeDtypeStruct(e, F32) for e in ends],
        name="widen",
    )(*made)
    one, two, down, up = (v[0] for v in outs[8:])
    return (*outs[:8], one, two, up, down)


def local(
    sizes,
    inputs,
    skip_in,
    lengths,
    cotangent,
    w_skip,
    gain_one,
    w_qkv,
    w_out,
    gain_two,
    w_up,
    b_up,
    w_down,
    b_down,
):
    n_u, n_z, n_x = sizes
    frames, d = inputs.shape
    hidden = w_up.shape[1]
    parts = n_u * n_x
    group = frames * parts
    u, z, x = (lax.axis_index(a) for a in AXES)
    me = u * n_x + x
    width = d // parts

    def line(a, b, c):
        return (a * n_z + b) * n_x + c

    def permute(v, to):
        pairs = [
            (line(a, b, c), line(*to(a, b, c)))
            for a in range(n_u)
            for b in range(n_z)
            for c in range(n_x)
        ]
        return lax.ppermute(v, AXES, pairs)

    def plane_of(a):
        return (a % 2) * (n_u // 2) + a // 2

    group_of = {plane_of(a): a for a in range(n_u)}

    def away(v):
        return permute(v, lambda a, b, c: (b, plane_of(a), c))

    def home(v):
        return permute(v, lambda a, b, c: (group_of[b], a, c))

    def swap_plane(v, bit):
        def to(a, b, c):
            other = (a * n_x + c) ^ bit
            return other // n_x, b, other % n_x

        return permute(v, to)

    plane_bits = [1 << i for i in range(parts.bit_length() - 1)]
    if n_x == 2 and n_u == 4:
        orders = ([1, 4, 2], [4, 1, 2])
    else:
        orders = (plane_bits, plane_bits)
    cut = frames // 32 * 16

    def gather_plane(v):
        pieces = []
        for piece, order in zip((v[:cut], v[cut:]), orders):
            for bit in order:
                piece = jnp.concatenate([piece, swap_plane(piece, bit)], axis=0)
            pieces.append(piece)
        return jnp.concatenate(pieces, axis=0)

    def gather_order(v):
        pieces = []
        for start, size, order in ((0, cut, orders[0]), (cut, frames - cut, orders[1])):
            offsets = [0]
            for bit in order:
                offsets = offsets + [o ^ bit for o in offsets]
            for o in offsets:
                pieces.append(
                    lax.dynamic_slice_in_dim(v, (me ^ o) * frames + start, size, axis=0)
                )
        return jnp.concatenate(pieces, axis=0)

    z_bits = n_z.bit_length() - 1

    def reduce_z(v):
        rest = v.shape[1:]
        v = v.reshape((2,) * z_bits + (v.shape[0] // n_z,) + rest)
        for bit in range(z_bits):
            axis = z_bits - 1 - bit
            own = (z >> bit) & 1
            keep = lax.dynamic_index_in_dim(v, own, axis, keepdims=False)
            give = lax.dynamic_index_in_dim(v, 1 - own, axis, keepdims=False)
            got = permute(
                give.astype(BF), lambda a, b, c, bit=bit: (a, b ^ (1 << bit), c)
            )
            v = keep.astype(F32) + got.astype(F32)
            if bit < z_bits - 1:
                v = v.astype(BF)
        return v.astype(BF)

    def finish_columns(v):
        if n_x == 2:
            v = v.reshape((2, v.shape[0] // 2) + v.shape[1:])
            keep = lax.dynamic_index_in_dim(v, x, 0, keepdims=False)
            give = lax.dynamic_index_in_dim(v, 1 - x, 0, keepdims=False)
            got = permute(give, lambda a, b, c: (a, b, 1 - c))
            both = jnp.where(x == 0, jnp.stack([keep, got]), jnp.stack([got, keep]))
        else:
            both = v[None]
        every = lax.all_gather(both, "u", axis=0)
        return every.reshape((parts,) + both.shape[1:])

    def sum_all(v):
        total = n_u * n_z * n_x
        for i in range(total.bit_length() - 1):
            bit = 1 << i
            pairs = [(n, n ^ bit) for n in range(total)]
            v = v + lax.ppermute(v, AXES, pairs)
        return v

    entry_home = dot_nn(inputs, w_skip[:d]) + dot_nn(skip_in, w_skip[d:])
    entry = away(entry_home.astype(BF)).astype(F32)
    group_lengths = away(lengths)[0]
    grad_low = away(cotangent)
    inputs_away = away(inputs)
    skip_away = away(skip_in)

    segment, places = frame_segments(group_lengths, jnp.arange(group, dtype=jnp.int32))
    own_places = lax.dynamic_slice_in_dim(places, me * frames, frames)
    tables = rotary_tables(own_places)
    col, row = segment[:, None], segment[None, :]

    inverse_one = rms_parts(entry)
    normed_one = (entry * inverse_one * gain_one).astype(BF)
    qkv = dot_nn(normed_one, w_qkv)
    query = (rotate(qkv[:, :d], tables, 1.0)).astype(BF) * BF(HEAD_DIM**-0.5)
    keys = rotate(qkv[:, d : 2 * d], tables, 1.0).astype(BF)
    values = qkv[:, 2 * d :].astype(BF)

    def to_heads(*arrays):
        n = len(arrays)
        v = jnp.stack([a.reshape(frames, parts, width) for a in arrays], axis=2)
        v = lax.all_to_all(
            v.reshape(frames, parts * n * width), PLANE, split_axis=1, concat_axis=0, tiled=True
        )
        return [v[:, i * width : (i + 1) * width] for i in range(n)]

    def to_frames(*arrays):
        n = len(arrays)
        v = jnp.concatenate(arrays, axis=1)
        v = lax.all_to_all(v, PLANE, split_axis=0, concat_axis=1, tiled=True)
        v = v.reshape(frames, parts, n, width)
        return [v[:, :, i].reshape(frames, d) for i in range(n)]

    head_query, head_keys, head_values = to_heads(query, keys, values)
    head_mixed, lse = call_forward(head_query, head_keys, head_values, col, row)
    (mixed,) = to_frames(head_mixed)

    middle = entry + dot_nn(mixed, w_out)
    inverse_two = rms_parts(middle)
    normed_two = (middle * inverse_two * gain_two).astype(BF)
    up = dot_nn(normed_two, w_up) + b_up
    d_active = dot_nt(grad_low, w_down)
    active, slope = gelu_both(up)
    d_up = (d_active * slope).astype(BF)
    result_away = (middle + dot_nn(active.astype(BF), w_down) + b_down).astype(BF)
    result = home(result_away)
    d_normed_two = dot_nt(d_up, w_up)
    middle_part, g_gain_two = rms_back(middle, inverse_two, gain_two, d_normed_two)
    d_middle = grad_low.astype(F32) + middle_part
    d_branch = d_middle.astype(BF)
    d_mixed = dot_nt(d_branch, w_out).astype(BF)
    (head_grad,) = to_heads(d_mixed)
    dq, dk, dv = call_backward(
        head_query, head_keys, head_values, head_mixed, head_grad, col, row, lse
    )

    chunk = hidden // (n_z * parts)
    w_up_own = lax.dynamic_slice(
        w_up.reshape(d, n_z, n_x, n_u, chunk), (0, 0, x, u, 0), (d, n_z, 1, 1, chunk)
    ).reshape(d, n_z * chunk)
    w_down_own = lax.dynamic_slice(
        w_down.reshape(n_z, n_x, n_u, chunk, d), (0, x, u, 0, 0), (n_z, 1, 1, chunk, d)
    ).reshape(n_z * chunk, d)
    b_up_own = lax.dynamic_slice(
        b_up.reshape(n_z, n_x, n_u, chunk), (0, x, u, 0), (n_z, 1, 1, chunk)
    ).reshape(n_z * chunk)
    plane_grad = gather_plane(grad_low)
    plane_normed = gather_plane(normed_two)
    up_own = dot_nn(plane_normed, w_up_own) + b_up_own
    active_own, slope_own = gelu_both(up_own)
    d_up_own = (dot_nt(plane_grad, w_down_own) * slope_own).astype(BF)
    g_down = dot_tn(active_own.astype(BF), plane_grad)
    g_up = dot_tn(plane_normed, d_up_own)
    down_z = reduce_z(g_down.astype(BF))
    up_z = reduce_z(g_up.astype(BF))
    out_down = lax.all_gather(down_z, "u", axis=0, tiled=True).astype(F32)
    out_up = finish_columns(up_z)
    out_up = (
        out_up.reshape(n_u, n_x, -1, n_z, chunk).transpose(2, 3, 1, 0, 4).reshape(-1, hidden)
    ).astype(F32)

    plane_mixed = gather_plane(mixed)
    own_branch = gather_order(
        lax.all_to_all(d_branch, PLANE, split_axis=1, concat_axis=0, tiled=True)
    )
    g_out = dot_tn(plane_mixed, own_branch)
    out_out = (
        finish_columns(reduce_z(g_out.astype(BF))).transpose(1, 0, 2).reshape(-1, d).astype(F32)
    )

    low = [a.astype(BF) for a in (dq, dk, dv)]
    frame_query, frame_keys, frame_values = to_frames(*low)
    d_qkv = jnp.concatenate(
        [
            rotate(frame_query.astype(F32), tables, -1.0).astype(BF),
            rotate(frame_keys.astype(F32), tables, -1.0).astype(BF),
            frame_values,
        ],
        axis=1,
    )
    d_normed_one = dot_nt(d_qkv, w_qkv)
    entry_part, g_gain_one = rms_back(entry, inverse_one, gain_one, d_normed_one)
    d_entry = (d_middle + entry_part).astype(BF)
    d_entry_home = home(d_entry)
    d_joined = dot_nt(d_entry_home, w_skip)
    d_inputs = d_joined[:, :d].astype(BF)
    d_skip = d_joined[:, d:].astype(BF)

    group_tables = rotary_tables(places)
    head_d_qkv = jnp.concatenate(
        [
            rotate(low[0].astype(F32), group_tables, -1.0).astype(BF),
            rotate(low[1].astype(F32), group_tables, -1.0).astype(BF),
            low[2],
        ],
        axis=1,
    )
    plane_first = gather_plane(normed_one)
    g_qkv = dot_tn(plane_first, gather_order(head_d_qkv))
    plane_inputs = gather_plane(inputs_away)
    plane_skip = gather_plane(skip_away)
    own_entry = gather_order(
        lax.all_to_all(d_entry, PLANE, split_axis=1, concat_axis=0, tiled=True)
    )
    g_skip = jnp.concatenate([dot_tn(plane_inputs, own_entry), dot_tn(plane_skip, own_entry)])
    out_qkv = finish_columns(reduce_z(g_qkv.astype(BF)))
    out_qkv = (
        out_qkv.reshape(parts, -1, 3, width).transpose(1, 2, 0, 3).reshape(-1, 3 * d).astype(F32)
    )
    out_skip = (
        finish_columns(reduce_z(g_skip.astype(BF))).transpose(1, 0, 2).reshape(-1, d).astype(F32)
    )

    early = sum_all(
        jnp.concatenate(
            [
                g_gain_two,
                jnp.sum(d_up.astype(F32), axis=0),
                jnp.sum(cotangent.astype(F32), axis=0),
            ]
        )
    )
    total_gain_one = sum_all(g_gain_one)
    return (
        result,
        d_inputs,
        d_skip,
        out_skip,
        total_gain_one,
        out_qkv,
        out_out,
        early[:d],
        out_up,
        early[d : d + hidden],
        out_down,
        early[d + hidden :],
    )


def local_fast(
    sizes,
    inputs,
    skip_in,
    lengths,
    cotangent,
    w_skip,
    gain_one,
    w_qkv,
    w_out,
    gain_two,
    w_up,
    b_up,
    w_down,
    b_down,
):
    made = call_layer(
        (inputs, skip_in, cotangent, w_skip, w_qkv, w_out, w_up, w_down),
        lengths,
        (gain_one[None], gain_two[None], b_up[None], b_down[None]),
    )
    (
        result,
        d_inputs,
        d_skip,
        g_skip,
        g_qkv,
        g_out,
        g_up,
        g_down,
        total_one,
        total_two,
        total_up,
        total_down,
    ) = call_widen(made)
    return (
        result,
        d_inputs,
        d_skip,
        g_skip,
        total_one,
        g_qkv,
        g_out,
        total_two,
        g_up,
        total_up,
        g_down,
        total_down,
    )


def solution(mesh):
    n_u, n_s = mesh.shape["utt"], mesh.shape["seq"]
    sizes = (n_u, n_u, n_s // n_u)
    program = local_fast if sizes == (4, 4, 2) else local
    inner = Mesh(mesh.devices.reshape(sizes), AXES)
    rows, seq = P(AXES, None), P(("z", "x"), None)
    in_specs = (rows, rows, P("u", None), rows) + (P(),) * 9
    out_specs = (rows, rows, rows, seq, P(), seq, seq, P(), seq, P(), seq, P())
    return jax.shard_map(
        functools.partial(program, sizes),
        mesh=inner,
        in_specs=in_specs,
        out_specs=out_specs,
        check_vma=False,
    )
```

profile of v0, /device:TPU:5, one launch (start us, length us, event | category | flops | bytes accessed | tf_op | source)
XLA Modules:
  0.0 213.4 jit_solution(5710544201810937542)
XLA Ops:
  0.6 204.1 %layer.1 = (bf16[176,1024]{1,0:T(8,128)(2,1)}, bf16[176,1024]{1,0:T(8,128)(2,1)}, bf16[176,1024]{1,0:T(8,128)(2,1)}, bf16[256,1024]{1,0:T(8,128)(2,1)}, bf16[128...) custom-call(s32[1,6]{1,0:T(1,128)} %lengths_ref.1, ...), custom_call_target="tpu_custom_call" | custom-call | tf_op jit(solution)/shard_map/layer/pallas_call | solution.py:1146
  204.8 8.4 %widen.1 = (bf16[176,1024]{1,0:T(8,128)(2,1)}, bf16[176,1024]{1,0:T(8,128)(2,1)}, bf16[176,1024]{1,0:T(8,128)(2,1)}, f32[256,1024]{1,0:T(8,128)}, f32[128,3072]{...) custom-call(bf16[176,1024]{1,0:T(8,128)(2,1)} %get-tuple-element.33., ...), custom_call_target="tpu_custom_call" | custom-call | tf_op jit(solution)/shard_map/widen/pallas_call | solution.py:1181
where the time goes:
time: 214 us; the launch traced here: 213 us
  Pallas kernels  213 us (100%)
    pallas_call x1, Pallas kernels, call_layer(): pl.pallas_call(layer_kernel, in_specs=[smem] + [vmem] * len(vectors) + [a...  204 us
    pallas_call x1, Pallas kernels, call_widen(): pl.pallas_call(widen_kernel, grid=(steps,), in_specs=whole[:3] + parts +...  8.43 us

commit v1 on v0

--- a/solution.py
+++ b/solution.py
@@ -74,7 +74,7 @@
 
 
 def backward_heads(
-    q_ref, k_ref, v_ref, o_ref, do_ref, col_ref, segment_row, lse_ref, dq_ref, dk_ref, dv_ref, acc
+    q_ref, k_ref, v_ref, o_ref, do_ref, col_ref, segment_row, lse_ref, dq_ref, dk_ref, dv_ref, acc, between=None
 ):
     frames, width = q_ref.shape
     heads = width // HEAD_DIM
@@ -122,6 +122,8 @@
             return 0
 
         lax.fori_loop(0, frames // block, step, 0)
+        if h == 0 and between is not None:
+            between()
     dq_ref[...] = acc[...].T * (HEAD_DIM**-0.5)
 
 
@@ -224,6 +226,17 @@
     return jnp.logical_and(a, b)
 
 
+def gelu_pair(t):
+    bell = jnp.exp(-0.5 * (t * t))
+    s = 1.0 / (1.0 + jnp.abs(t) * (0.3275911 * 0.7071067811865476))
+    tail = 0.5 * 1.061405429 * s - 0.5 * 1.453152027
+    tail = tail * s + 0.5 * 1.421413741
+    tail = tail * s - 0.5 * 0.284496736
+    tail = (tail * s + 0.5 * 0.254829592) * s * bell
+    below = jnp.where(t < 0.0, tail, 1.0 - tail)
+    return t * below, below + t * (0.3989422804014327 * bell)
+
+
 def rms_back_rows(hidden, inverse, gain, grad):
     scaled = hidden * inverse
     weighted = grad * gain
@@ -280,13 +293,20 @@
     def finish(self):
         for copy in self.sent:
             copy.wait_send()
-        for copy, own in self.kept:
-
-            @pl.when(jnp.logical_not(own))
-            def _(copy=copy):
-                copy.wait_send()
-
+        settle(self.kept)
         self.sent, self.kept = [], []
+
+    def take(self, n):
+        taken, self.kept = self.kept[-n:], self.kept[:-n]
+        return taken
+
+
+def settle(kept):
+    for copy, own in kept:
+
+        @pl.when(jnp.logical_not(own))
+        def _(copy=copy):
+            copy.wait_send()
 
 
 def plane_peers(u, z, x):
@@ -308,32 +328,33 @@
         self.sender, self.buffer, self.peers = sender, buffer, peers
         self.first, self.size = start, size
         self.low = size // 32 * 16
-        self.copies = []
-
-    def pass_on(self, k, to, start=0, size=None):
+        self.x, self.y = self.copy(0, 1), self.copy(0, 4)
+        self.over_y = self.copy(1, 4, self.low, size - self.low)
+        self.over_x = self.copy(4, 1, 0, self.low)
+        self.cores = [self.copy(k, 2) for k in (0, 1, 4, 5)]
+        self.copies = [self.x, self.y, self.over_x, self.over_y] + self.cores
+
+    def copy(self, k, to, start=0, size=None):
         rows = rows_of(self.peers[k][1], self.first + start, size or self.size)
-        copy = self.sender.remote(self.buffer.at[rows], self.buffer.at[rows], self.peers[to][0])
-        copy.start()
-        self.copies.append(copy)
-        return copy
+        return self.sender.remote(self.buffer.at[rows], self.buffer.at[rows], self.peers[to][0])
 
     def start(self):
-        self.x = self.pass_on(0, 1)
-        self.y = self.pass_on(0, 4)
-        self.cores = [self.pass_on(0, 2)]
+        self.x.start()
+        self.y.start()
+        self.cores[0].start()
 
     def forward(self):
         self.x.wait_recv()
-        self.over_y = self.pass_on(1, 4, self.low, self.size - self.low)
-        self.cores.append(self.pass_on(1, 2))
+        self.over_y.start()
+        self.cores[1].start()
         self.y.wait_recv()
-        self.over_x = self.pass_on(4, 1, 0, self.low)
-        self.cores.append(self.pass_on(4, 2))
+        self.over_x.start()
+        self.cores[2].start()
 
     def corner(self):
         self.over_x.wait_recv()
         self.over_y.wait_recv()
-        self.cores.append(self.pass_on(5, 2))
+        self.cores[3].start()
 
     def core(self, i):
         self.cores[i].wait_recv()
@@ -472,8 +493,8 @@
     seg,
     entry,
     middle,
-    down_sum,
-    normed_sum,
+    dq,
+    dk,
     result,
     result_r,
     d_mixed,
@@ -485,6 +506,7 @@
     gq,
     gs,
     go,
+    d_up,
     d1,
     d2,
     d3,
@@ -537,6 +559,26 @@
     sender = Sender(send, recv, load)
     mine = rows_of(me)
     low, high = 80, 96
+    z_devices = (
+        (u, flip_low(z), x),
+        (u, flip_high(z), x),
+        (u, flip_low(flip_high(z)), x),
+    )
+
+    barrier = pltpu.get_barrier_semaphore()
+
+    def greet(device):
+        pl.semaphore_signal(barrier, inc=1, device_id=device, device_id_type=MESH_ID)
+
+    for device, _ in peers[1:]:
+        greet(device)
+    for device in z_devices:
+        greet(device)
+
+    @pl.when(jnp.logical_not(stays_away))
+    def _():
+        greet(away)
+        greet(home)
 
     got_x = sender.local(inputs_ref, gd.at[pl.ds(0, TOK)])
     got_s = sender.local(skip_ref, gd.at[pl.ds(TOK, TOK)])
@@ -554,24 +596,23 @@
     for s in range(slots):
         lens[s : s + 1, :] = jnp.full((1, 128), lengths_ref[0, s].astype(F32), F32)
     lens[slots:8, :] = jnp.zeros((8 - slots, 128), F32)
-    sent_lens = sender.push_or_keep(lens, lens_r, away, stays_away)
     got_x.wait()
     got_w[0].wait()
     value = dot_nn(gd[:TOK, :], wide_b[:d, :])
     got_s.wait()
     got_w[1].wait()
     d_mixed[...] = (value + dot_nn(gd[TOK : 2 * TOK, :], wide_b[d : 2 * d, :])).astype(BF)
+    pl.semaphore_wait(barrier, jnp.where(stays_away, 10, 12))
     sent_entry = [
         sender.push_or_keep(
             d_mixed.at[pl.ds(a, n)], entry.at[pl.ds(a, n)], away, stays_away
         )
         for a, n in ((0, low), (low, high))
     ]
+    entry_left = sender.take(2)
+    sent_lens = sender.push_or_keep(lens, lens_r, away, stays_away)
     got_down = sender.local(w_down_ref, wide_b)
     got_out = sender.local(w_out_ref, w_out)
-
-    def joined_block(j):
-        return slice(j // 2 * TOK, (j // 2 + 1) * TOK), slice(j % 2 * 256, (j % 2 + 1) * 256)
 
     lane = lax.broadcasted_iota(jnp.int32, (TOK, 128), 1)
     for a in range(4):
@@ -591,6 +632,25 @@
                     j // 2 * TOK : (j // 2 + 1) * TOK,
                     j % 2 * 256 + pair * 128 : j % 2 * 256 + (pair + 1) * 128,
                 ] = jnp.where(lane < 64, halves[0], halves[1]).astype(BF)
+
+    def joined_for(a, b):
+        return gu.at[
+            pl.ds(pl.multiple_of(a * TOK, 16), TOK), pl.ds(pl.multiple_of(b * 256, 256), 256)
+        ]
+
+    def joined_from(a, b):
+        first = lax.rem(a, 2) * 512 + b * 256
+        return fin_d.at[
+            pl.ds(pl.multiple_of(lax.div(a, 2) * TOK, 16), TOK),
+            pl.ds(pl.multiple_of(first, 256), 256),
+        ]
+
+    own_joined = sender.local(joined_for(u, x), joined_from(u, x))
+    got_joined = []
+    for device, _ in peers[1:]:
+        copy = sender.remote(joined_for(device[0], device[2]), joined_from(u, x), device)
+        copy.start()
+        got_joined.append(copy)
 
     sent_lens.wait_recv()
     freqs = jnp.exp(lax.rem(lane, 32).astype(F32) * (-2.0 * math.log(10000.0) / HEAD_DIM))
@@ -669,16 +729,20 @@
     sent_cot.wait_recv()
     gather_cot = PlaneGather(sender, ct, peers)
     gather_cot.start()
+    own_joined.wait()
+    for copy in got_joined:
+        copy.wait_recv()
     for a in range(4):
+        to = a % 2 * 2 + a // 2
         for b in range(2):
-            rows, cols = joined_block(2 * a + b)
             sender.push_or_keep(
-                gu.at[rows, cols],
-                joined.at[rows_of(2 * z + x)],
-                (a, plane, b),
-                both(both(u == a, x == b), plane == z),
-                spread.at[2 * z + x],
+                joined_from(jnp.int32(a), jnp.int32(b)),
+                joined.at[rows_of(2 * z + b)],
+                (u, jnp.int32(to), x),
+                z == to,
+                spread.at[2 * z + b],
             )
+    joined_left = sender.take(8)
 
     pl.run_scoped(
         lambda out_t: forward_heads(q, k, v, seg, segment_row, o, lse, acc, out_t),
@@ -693,6 +757,15 @@
         for i in range(1, 8)
     ]
     gather_cot.forward()
+    got_down.wait()
+    step = d
+
+    def back_feed(c, _):
+        cols = pl.ds(pl.multiple_of(c * step, step), step)
+        db[rows_of(c), :] = dot_nt(ct[mine, :], wide_b[cols, :]).astype(BF)
+        return 0
+
+    lax.fori_loop(0, hidden // step, back_feed, 0)
     own_mixed.wait()
     for copy in got_mixed:
         copy.wait_recv()
@@ -704,20 +777,28 @@
     gather_normed = PlaneGather(sender, n2, peers)
     gather_normed.start()
 
-    down_sum[...] = jnp.zeros_like(down_sum)
-    normed_sum[...] = jnp.zeros_like(normed_sum)
+    dq[...] = jnp.zeros_like(dq)
+    dk[...] = jnp.zeros_like(dk)
+
+    def add_to(ref, value):
+        for j in range(d // 128):
+            ref[j * TOK : (j + 1) * TOK, :] += value[:, j * 128 : (j + 1) * 128]
+
+    def side_by_side(ref):
+        return jnp.concatenate([ref[j * TOK : (j + 1) * TOK, :] for j in range(d // 128)], axis=1)
+
     got_up.wait()
-    got_down.wait()
-    step = 512
 
     def feed(c, _):
         cols = pl.ds(pl.multiple_of(c * step, step), step)
         up = dot_nn(n2[mine, :], wide_a[:, cols]) + b_up_ref[:, cols]
-        active, slope = gelu_both(up)
-        d_up = (dot_nt(ct[mine, :], wide_b[cols, :]) * slope).astype(BF)
-        down_sum[...] += dot_nn(active.astype(BF), wide_b[cols, :])
-        normed_sum[...] += dot_nt(d_up, wide_a[:, cols])
-        vec[pl.ds(8 + c, 1), :] = jnp.sum(d_up.astype(F32), axis=0, keepdims=True)
+        active, slope = gelu_pair(up)
+        d_up = (db[rows_of(c), :].astype(F32) * slope).astype(BF)
+        add_to(dq, dot_nn(active.astype(BF), wide_b[cols, :]))
+        add_to(dk, dot_nt(d_up, wide_a[:, cols]))
+        sums = jnp.sum(d_up.astype(F32), axis=0, keepdims=True)
+        vec[pl.ds(8 + 2 * c, 1), :] = sums[:, : step // 2]
+        vec[pl.ds(9 + 2 * c, 1), :] = sums[:, step // 2 :]
         return 0
 
     half = hidden // step // 2
@@ -727,19 +808,13 @@
     gather_normed.forward()
     value = middle[...]
     inverse = rms_parts(value)
-    back, g_gain_two = rms_back_rows(value, inverse, gain_two_ref[...], normed_sum[...])
+    back, g_gain_two = rms_back_rows(value, inverse, gain_two_ref[...], side_by_side(dk))
     grad_out = ct[mine, :].astype(F32)
     d_middle = grad_out + back
-    result[...] = (value + down_sum[...] + b_down_ref[...]).astype(BF)
+    result[...] = (value + side_by_side(dq) + b_down_ref[...]).astype(BF)
     middle[...] = d_middle
     db[mine, :] = d_middle.astype(BF)
-    for copy, own in sender.kept[1:3]:
-
-        @pl.when(jnp.logical_not(own))
-        def _(copy=copy):
-            copy.wait_send()
-
-    sender.kept = sender.kept[:1] + sender.kept[3:]
+    settle(entry_left)
     d_mixed[...] = dot_nt(db[mine, :], w_out[...]).astype(BF)
     own_grad = sender.local(d_mixed.at[:, heads_at], grad.at[mine])
     got_grad = [
@@ -756,57 +831,42 @@
         part = slice(i * d // 2, (i + 1) * d // 2)
         vec[2 + i : 3 + i, :] = g_gain_two[:, part]
         vec[4 + i : 5 + i, :] = g_b_down[:, part]
-    vec[6:8, :] = jnp.zeros((2, step), F32)
+    vec[6:8, :] = jnp.zeros((2, d // 2), F32)
     gather_cot.done()
-    gather_normed.corner()
-    gather_branch = PlaneGather(sender, db, peers)
-    gather_branch.start()
-    gather_normed.done()
-    for j in range(8):
-        rows, cols = joined_block(j)
-        copy, own = sender.kept[2 + j]
-
-        @pl.when(jnp.logical_not(own))
-        def _(copy=copy):
-            copy.wait_send()
-
-    sender.kept = sender.kept[:2] + sender.kept[10:]
-    for s in range(8):
-        rows = pl.ds(s * TOK, TOK)
-        pltpu.make_async_copy(joined.at[rows], joined.at[rows], spread.at[s]).wait()
 
     chunk = hidden // 32
     sum_down = PlaneSum(sender, gd, d1, d2, d3, place)
     sum_up = PlaneSum(sender, gu, u1, u2, u3, place)
-
-    def own_units(w_up_own, w_down_own, active, d_up):
-        copies, starts = [], []
-        for s in range(4):
-            first = pl.multiple_of((2 * s + x) * (4 * chunk) + u * chunk, chunk)
-            starts.append(first)
-            copies.append(
-                sender.local(
-                    w_up_ref.at[:, pl.ds(first, chunk)], w_up_own.at[:, pl.ds(s * chunk, chunk)]
-                )
-            )
-            copies.append(
-                sender.local(
-                    w_down_ref.at[pl.ds(first, chunk)], w_down_own.at[pl.ds(s * chunk, chunk)]
-                )
-            )
-        for copy in copies:
-            copy.wait()
+    gather_branch = PlaneGather(sender, db, peers)
+
+    def own_units(w_up_own, w_down_own, active):
+        starts = [
+            pl.multiple_of((2 * s + x) * (4 * chunk) + u * chunk, chunk) for s in range(4)
+        ]
+        for s, first in enumerate(starts):
+            part = slice(s * chunk, (s + 1) * chunk)
+            w_up_own[:, part] = wide_a[:, pl.ds(first, chunk)]
+            w_down_own[part, :] = wide_b[pl.ds(first, chunk), :]
         bias = jnp.concatenate([b_up_ref[:, pl.ds(first, chunk)] for first in starts], axis=1)
 
-        def units(i, _):
-            rows = rows_of(i)
+        def units(i):
+            rows = pl.ds(pl.multiple_of(peers[i][0][0] * (2 * TOK), 16), 2 * TOK)
             up = dot_nn(n2[rows, :], w_up_own[...]) + bias
-            act, slope = gelu_both(up)
+            act, slope = gelu_pair(up)
             active[rows, :] = act.astype(BF)
             d_up[rows, :] = (dot_nt(ct[rows, :], w_down_own[...]) * slope).astype(BF)
-            return 0
-
-        lax.fori_loop(0, group // TOK, units, 0)
+
+        units(0)
+        gather_normed.corner()
+        gather_normed.core(0)
+        gather_normed.core(1)
+        units(2)
+        units(4)
+        gather_normed.core(2)
+        gather_normed.core(3)
+        units(6)
+        gather_normed.left()
+        gather_branch.start()
 
         def down_terms(i, _):
             cols = pl.ds(pl.multiple_of(i * 256, 256), 256)
@@ -815,32 +875,22 @@
 
         lax.fori_loop(0, 4 * chunk // 256, down_terms, 0)
         sum_down.start()
-
-        def up_terms(i, _):
-            cols = pl.ds(pl.multiple_of(i * 256, 256), 256)
-            gu[cols, :] = dot_tn(n2[:, cols], d_up[...]).astype(BF)
-            return 0
-
-        lax.fori_loop(0, d // 256, up_terms, 0)
-        sum_up.start()
 
     pl.run_scoped(
         own_units,
         pltpu.VMEM((d, 4 * chunk), BF),
         pltpu.VMEM((4 * chunk, d), BF),
         pltpu.VMEM((group, 4 * chunk), BF),
-        pltpu.VMEM((group, 4 * chunk), BF),
     )
     got_normed = sender.local(normed_kept, ct)
     got_qkv = sender.local(w_qkv_ref, wide_a.at[:, pl.ds(0, 3 * d)])
     got_skip = sender.local(w_skip_ref, wide_b.at[pl.ds(0, 2 * d)])
-    gather_branch.forward()
     own_grad.wait()
     for copy in got_grad:
         copy.wait_recv()
 
-    def heads(dq, dk, dv):
-        backward_heads(q, k, v, o, grad, seg, lse[2:3, :], lse, dq, dk, dv, acc)
+    def heads(dv):
+        backward_heads(q, k, v, o, grad, seg, lse[2:3, :], lse, dq, dk, dv, acc, gather_branch.forward)
 
         def turn_back(i, _):
             rows = rows_of(i)
@@ -852,7 +902,10 @@
 
         lax.fori_loop(0, group // TOK, turn_back, 0)
 
-    pl.run_scoped(heads, *[pltpu.VMEM((group, 128), F32)] * 3)
+    pl.run_scoped(heads, pltpu.VMEM((group, 128), F32))
+    settle(joined_left)
+    for copy in got_joined:
+        copy.wait_send()
     own_frames = sender.local(d_heads.at[:, mine], d_frames.at[:, :, heads_at])
     got_frames = [
         sender.push(
@@ -861,6 +914,14 @@
         for i in range(1, 8)
     ]
     gather_branch.corner()
+
+    def up_terms(i, _):
+        cols = pl.ds(pl.multiple_of(i * 256, 256), 256)
+        gu[cols, :] = dot_tn(n2[:, cols], d_up[...]).astype(BF)
+        return 0
+
+    lax.fori_loop(0, d // 256, up_terms, 0)
+    sum_up.start()
     got_normed.wait()
 
     def qkv_terms(i, _):
@@ -882,12 +943,11 @@
     to_far = sender.remote(go, o1, (u, flip_high(z), x))
     to_near = sender.remote(go, o2, (u, flip_low(z), x))
 
-    @pl.when(jnp.logical_not(same_high))
+    @pl.when(jnp.logical_not(same_low))
     def _():
-        to_far.start()
+        to_near.start()
 
     sum_down.middle()
-    sum_up.middle()
 
     own_frames.wait()
     for copy in got_frames:
@@ -898,10 +958,12 @@
     d_normed += dot_nt(d_frames[2], wide_a[:, 2 * d : 3 * d])
     value = entry[...].astype(F32)
     back, g_gain_one = rms_back_rows(value, rms_parts(value), gain_one_ref[...], d_normed)
-    n2[mine, :] = (middle[...] + back).astype(BF)
-    gather_entry = PlaneGather(sender, n2, peers)
+    wide_b[rows_of(me, 2 * d), :] = (middle[...] + back).astype(BF)
+    gather_entry = PlaneGather(sender, wide_b, peers, 2 * d)
     gather_entry.start()
-    sent_back = sender.push_or_keep(n2.at[mine], entry_r, home, stays_home)
+    sent_back = sender.push_or_keep(
+        wide_b.at[rows_of(me, 2 * d)], entry_r, home, stays_home
+    )
 
     for i in range(2):
         vec[i : i + 1, :] = g_gain_one[:, i * d // 2 : (i + 1) * d // 2]
@@ -909,22 +971,18 @@
     got_vec = [sender.push(vec, vec_plane.at[vec_at], peers[i][0]) for i in range(1, 8)]
     vec_plane[vec_at, :] = vec[...]
 
+    sum_up.middle()
+    for s in range(8):
+        rows = pl.ds(s * TOK, TOK)
+        pltpu.make_async_copy(joined.at[rows], joined.at[rows], spread.at[s]).wait()
     def skip_terms(i):
-        rows = rows_of(peers[i][1])
-        return dot_tn(joined[rows, :], n2[rows, :])
+        p = peers[i][1]
+        return dot_tn(joined[rows_of(p), :], wide_b[rows_of(p, 2 * d), :])
 
     total = skip_terms(0)
 
-    @pl.when(same_high)
-    def _():
-        to_far.wait_recv()
-        go[...] = (go[...].astype(F32) + o1[...].astype(F32)).astype(BF)
-
-    @pl.when(both(same_high, jnp.logical_not(same_low)))
-    def _():
-        to_near.start()
-
     gather_entry.forward()
+    sum_qkv.middle()
     total += skip_terms(1)
     total += skip_terms(4)
     gather_entry.corner()
@@ -937,18 +995,21 @@
     sum_skip = PlaneSum(sender, gs, s1, s2, s3, place)
     sum_skip.start()
 
-    sum_qkv.middle()
+    @pl.when(same_low)
+    def _():
+        to_near.wait_recv()
+        go[...] = (go[...].astype(F32) + o2[...].astype(F32)).astype(BF)
+
+    @pl.when(both(same_low, jnp.logical_not(same_high)))
+    def _():
+        to_far.start()
+
     for copy in got_vec:
         copy.wait_recv()
     value = vec_plane[0:16, :]
     for i in range(1, 8):
         value += vec_plane[16 * i : 16 * (i + 1), :]
     vec_sum[...] = value
-    z_devices = (
-        (u, flip_low(z), x),
-        (u, flip_high(z), x),
-        (u, flip_low(flip_high(z)), x),
-    )
     vec_at = pl.ds(pl.multiple_of(z * 16, 16), 16)
     got_vec = [sender.push(vec_sum, vec_z.at[vec_at], device) for device in z_devices]
     vec_z[vec_at, :] = vec_sum[...]
@@ -971,8 +1032,8 @@
 
     @pl.when(owner)
     def _():
-        to_near.wait_recv()
-        fin_o[...] = (go[...].astype(F32) + o2[...].astype(F32)).astype(BF)
+        to_far.wait_recv()
+        fin_o[...] = (go[...].astype(F32) + o1[...].astype(F32)).astype(BF)
 
     def tell(i, to):
         return pltpu.make_async_remote_copy(
@@ -1045,13 +1106,13 @@
     def _():
         tell_on.wait_send()
 
-    @pl.when(jnp.logical_not(same_high))
+    @pl.when(jnp.logical_not(same_low))
+    def _():
+        to_near.wait_send()
+
+    @pl.when(both(same_low, jnp.logical_not(same_high)))
     def _():
         to_far.wait_send()
-
-    @pl.when(both(same_high, jnp.logical_not(same_low)))
-    def _():
-        to_near.wait_send()
 
     last_skip.done()
     outs.append(sender.local(fin_s, g_skip_out))
@@ -1111,8 +1172,8 @@
         table,
         block,
         total,
-        total,
-        total,
+        table,
+        table,
         block,
         block,
         block,
@@ -1124,6 +1185,7 @@
         ((d, 384), BF),
         ((256, d), BF),
         ((128, d), BF),
+        ((group, unit), BF),
         *sums(unit // 4, d),
         *sums(d // 4, unit),
         *sums(d // 4, 384),
@@ -1152,7 +1214,7 @@
         + [pltpu.SemaphoreType.DMA((160,))] * 3
         + [pltpu.SemaphoreType.DMA((12,))],
         compiler_params=pltpu.CompilerParams(
-            vmem_limit_bytes=60 * 2**20 + 2**18, has_side_effects=True
+            vmem_limit_bytes=60 * 2**20 + 2**18, has_side_effects=True, collective_id=0
         ),
         name="layer",
     )(lengths, *vectors, *arrays)

time: 214 us -> 198 us (0.925)
  Pallas kernels: 213 us -> 197 us
    pallas_call x1, Pallas kernels: 204 us -> 188 us  [call_layer(): pl.pallas_call(layer_kernel, in_specs=[smem] + [vmem] * len(vectors) + [a...]
where the time goes in v1:
time: 198 us
  Pallas kernels  197 us (99%)
    pallas_call x1, Pallas kernels, call_layer(): pl.pallas_call(layer_kernel, in_specs=[smem] + [vmem] * len(vectors) + [a...  188 us
    pallas_call x1, Pallas kernels, call_widen(): pl.pallas_call(widen_kernel, grid=(steps,), in_specs=whole[:3] + parts +...  8.43 us

profile of v1, /device:TPU:5, one launch (start us, length us, event | category | flops | bytes accessed | tf_op | source)
XLA Modules:
  0.0 197.7 jit_solution(10902026722007063106)
XLA Ops:
  0.6 188.5 %layer.1 = (bf16[176,1024]{1,0:T(8,128)(2,1)}, bf16[176,1024]{1,0:T(8,128)(2,1)}, bf16[176,1024]{1,0:T(8,128)(2,1)}, bf16[256,1024]{1,0:T(8,128)(2,1)}, bf16[128...) custom-call(s32[1,6]{1,0:T(1,128)} %lengths_ref.1, ...), custom_call_target="tpu_custom_call" | custom-call | tf_op jit(solution)/shard_map/layer/pallas_call | solution.py:1208
  189.1 8.4 %widen.1 = (bf16[176,1024]{1,0:T(8,128)(2,1)}, bf16[176,1024]{1,0:T(8,128)(2,1)}, bf16[176,1024]{1,0:T(8,128)(2,1)}, f32[256,1024]{1,0:T(8,128)}, f32[128,3072]{...) custom-call(bf16[176,1024]{1,0:T(8,128)(2,1)} %get-tuple-element.33., ...), custom_call_target="tpu_custom_call" | custom-call | tf_op jit(solution)/shard_map/widen/pallas_call | solution.py:1243

commit v2 on v1

--- a/solution.py
+++ b/solution.py
@@ -688,13 +688,17 @@
         return t * cos_t[rows, :] + swapped * (way * sin_t[rows, :])
 
     def project(i):
-        rows = rows_of(peers[i][1])
+        first = peers[i][0][0] * (2 * TOK)
+        rows = pl.ds(pl.multiple_of(first, 16), 2 * TOK)
         value = dot_nn(n2[rows, :], wide_a[:, :384])
-        q[rows, :] = (
-            turn(value[:, :128], rows, 1.0).astype(BF).astype(F32) * HEAD_DIM**-0.5
-        ).astype(BF)
-        k[rows, :] = turn(value[:, 128:256], rows, 1.0).astype(BF)
-        v[rows, :] = value[:, 256:].astype(BF)
+        for h in range(2):
+            rows = pl.ds(pl.multiple_of(first + h * TOK, 16), TOK)
+            part = value[h * TOK : (h + 1) * TOK]
+            q[rows, :] = (
+                turn(part[:, :128], rows, 1.0).astype(BF).astype(F32) * HEAD_DIM**-0.5
+            ).astype(BF)
+            k[rows, :] = turn(part[:, 128:256], rows, 1.0).astype(BF)
+            v[rows, :] = part[:, 256:].astype(BF)
 
     first_a = PlaneGather(sender, n2, peers, 0, low)
     first_b = PlaneGather(sender, n2, peers, low, high)
@@ -705,25 +709,19 @@
         gather.start()
     sent_cot = sender.push_or_keep(cot_ref, ct.at[rows_of(2 * z + x)], away, stays_away)
     first_a.forward()
+    first_b.forward()
     project(0)
-    first_a.core(0)
-    first_b.core(0)
+    for gather in (first_a, first_b):
+        gather.core(0)
+        gather.core(1)
     project(2)
-    first_b.forward()
-    project(1)
-    project(4)
     first_a.corner()
     first_b.corner()
-    project(5)
-    for gather in (first_a, first_b):
-        gather.core(1)
-    project(3)
+    project(4)
     for gather in (first_a, first_b):
         gather.core(2)
+        gather.core(3)
     project(6)
-    for gather in (first_a, first_b):
-        gather.core(3)
-    project(7)
     got_up = sender.local(w_up_ref, wide_a)
     kept_normed = sender.local(n2, normed_kept)
     sent_cot.wait_recv()
@@ -774,8 +772,10 @@
     value = entry[...].astype(F32) + dot_nn(d_frames[0], w_out[...])
     middle[...] = value
     n2[mine, :] = (value * rms_parts(value) * gain_two_ref[...]).astype(BF)
-    gather_normed = PlaneGather(sender, n2, peers)
-    gather_normed.start()
+    normed_a = PlaneGather(sender, n2, peers, 0, low)
+    normed_b = PlaneGather(sender, n2, peers, low, high)
+    normed_a.start()
+    normed_b.start()
 
     dq[...] = jnp.zeros_like(dq)
     dk[...] = jnp.zeros_like(dk)
@@ -805,7 +805,8 @@
     lax.fori_loop(0, half, feed, 0)
     gather_cot.corner()
     lax.fori_loop(half, 2 * half, feed, 0)
-    gather_normed.forward()
+    normed_a.forward()
+    normed_b.forward()
     value = middle[...]
     inverse = rms_parts(value)
     back, g_gain_two = rms_back_rows(value, inverse, gain_two_ref[...], side_by_side(dk))
@@ -825,7 +826,6 @@
         )
         for i in range(1, 8)
     ]
-    sent_result = sender.push_or_keep(result, result_r, home, stays_home)
     g_b_down = jnp.sum(grad_out, axis=0, keepdims=True)
     for i in range(2):
         part = slice(i * d // 2, (i + 1) * d // 2)
@@ -857,15 +857,21 @@
             d_up[rows, :] = (dot_nt(ct[rows, :], w_down_own[...]) * slope).astype(BF)
 
         units(0)
-        gather_normed.corner()
-        gather_normed.core(0)
-        gather_normed.core(1)
+        normed_a.corner()
+        normed_b.corner()
+        normed_a.core(0)
+        normed_b.core(0)
+        normed_a.core(1)
+        normed_b.core(1)
         units(2)
         units(4)
-        gather_normed.core(2)
-        gather_normed.core(3)
+        normed_a.core(2)
+        normed_b.core(2)
+        normed_a.core(3)
+        normed_b.core(3)
         units(6)
-        gather_normed.left()
+        normed_a.left()
+        normed_b.left()
         gather_branch.start()
 
         def down_terms(i, _):
@@ -888,6 +894,7 @@
     own_grad.wait()
     for copy in got_grad:
         copy.wait_recv()
+    sent_result = sender.push_or_keep(result, result_r, home, stays_home)
 
     def heads(dv):
         backward_heads(q, k, v, o, grad, seg, lse[2:3, :], lse, dq, dk, dv, acc, gather_branch.forward)
@@ -959,8 +966,10 @@
     value = entry[...].astype(F32)
     back, g_gain_one = rms_back_rows(value, rms_parts(value), gain_one_ref[...], d_normed)
     wide_b[rows_of(me, 2 * d), :] = (middle[...] + back).astype(BF)
-    gather_entry = PlaneGather(sender, wide_b, peers, 2 * d)
-    gather_entry.start()
+    entry_a = PlaneGather(sender, wide_b, peers, 2 * d, low)
+    entry_b = PlaneGather(sender, wide_b, peers, 2 * d + low, high)
+    entry_a.start()
+    entry_b.start()
     sent_back = sender.push_or_keep(
         wide_b.at[rows_of(me, 2 * d)], entry_r, home, stays_home
     )
@@ -981,13 +990,15 @@
 
     total = skip_terms(0)
 
-    gather_entry.forward()
+    entry_a.forward()
+    entry_b.forward()
     sum_qkv.middle()
     total += skip_terms(1)
     total += skip_terms(4)
-    gather_entry.corner()
+    entry_a.corner()
+    entry_b.corner()
     total += skip_terms(5)
-    for copy in gather_entry.cores:
+    for copy in entry_a.cores + entry_b.cores:
         copy.wait_recv()
     for i in (2, 3, 6, 7):
         total += skip_terms(i)
@@ -1118,7 +1129,8 @@
     outs.append(sender.local(fin_s, g_skip_out))
     for copy in outs:
         copy.wait()
-    gather_entry.left()
+    entry_a.left()
+    entry_b.left()
     sender.finish()
 
 
@@ -1233,7 +1245,7 @@
 
 
 def call_widen(made):
-    steps = 8
+    steps = 4
     whole = [pl.BlockSpec(a.shape, lambda i: (0, 0)) for a in made]
     parts = [
         pl.BlockSpec((a.shape[0] // steps, a.shape[1]), lambda i: (i, 0)) for a in made[3:8]

time: 198 us -> 195 us (0.985)
  Pallas kernels: 197 us -> 194 us
    pallas_call x1, Pallas kernels: 8.43 us -> 6.35 us  [call_widen(): pl.pallas_call(widen_kernel, grid=(steps,), in_specs=whole[:3] + parts +...]
where the time goes in v2:
time: 195 us
  Pallas kernels  194 us (99%)
    pallas_call x1, Pallas kernels, call_layer(): pl.pallas_call(layer_kernel, in_specs=[smem] + [vmem] * len(vectors) + [a...  188 us
    pallas_call x1, Pallas kernels, call_widen(): pl.pallas_call(widen_kernel, grid=(steps,), in_specs=whole[:3] + parts +...  6.35 us

profile of v2, /device:TPU:5, one launch (start us, length us, event | category | flops | bytes accessed | tf_op | source)
XLA Modules:
  0.0 195.2 jit_solution(14482613375243891398)
XLA Ops:
  0.6 188.0 %layer.1 = (bf16[176,1024]{1,0:T(8,128)(2,1)}, bf16[176,1024]{1,0:T(8,128)(2,1)}, bf16[176,1024]{1,0:T(8,128)(2,1)}, bf16[256,1024]{1,0:T(8,128)(2,1)}, bf16[128...) custom-call(s32[1,6]{1,0:T(1,128)} %lengths_ref.1, ...), custom_call_target="tpu_custom_call" | custom-call | tf_op jit(solution)/shard_map/layer/pallas_call | solution.py:1220
  188.6 6.3 %widen.1 = (bf16[176,1024]{1,0:T(8,128)(2,1)}, bf16[176,1024]{1,0:T(8,128)(2,1)}, bf16[176,1024]{1,0:T(8,128)(2,1)}, f32[256,1024]{1,0:T(8,128)}, f32[128,3072]{...) custom-call(bf16[176,1024]{1,0:T(8,128)(2,1)} %get-tuple-element.33., ...), custom_call_target="tpu_custom_call" | custom-call | tf_op jit(solution)/shard_map/widen/pallas_call | solution.py:1255

commit v3 on v2

--- a/solution.py
+++ b/solution.py
@@ -970,9 +970,6 @@
     entry_b = PlaneGather(sender, wide_b, peers, 2 * d + low, high)
     entry_a.start()
     entry_b.start()
-    sent_back = sender.push_or_keep(
-        wide_b.at[rows_of(me, 2 * d)], entry_r, home, stays_home
-    )
 
     for i in range(2):
         vec[i : i + 1, :] = g_gain_one[:, i * d // 2 : (i + 1) * d // 2]
@@ -1006,6 +1003,9 @@
     sum_skip = PlaneSum(sender, gs, s1, s2, s3, place)
     sum_skip.start()
 
+    sent_back = sender.push_or_keep(
+        wide_b.at[rows_of(me, 2 * d)], entry_r, home, stays_home
+    )
     @pl.when(same_low)
     def _():
         to_near.wait_recv()

time: 195 us -> 193 us (0.990)
  Pallas kernels: 194 us -> 192 us
    pallas_call x1, Pallas kernels: 188 us -> 186 us  [call_layer(): pl.pallas_call(layer_kernel, in_specs=[smem] + [vmem] * len(vectors) + [a...]
where the time goes in v3:
time: 193 us
  Pallas kernels  192 us (99%)
    pallas_call x1, Pallas kernels, call_layer(): pl.pallas_call(layer_kernel, in_specs=[smem] + [vmem] * len(vectors) + [a...  186 us
    pallas_call x1, Pallas kernels, call_widen(): pl.pallas_call(widen_kernel, grid=(steps,), in_specs=whole[:3] + parts +...  6.35 us

profile of v3, /device:TPU:5, one launch (start us, length us, event | category | flops | bytes accessed | tf_op | source)
XLA Modules:
  0.0 192.9 jit_solution(9344655453899211240)
XLA Ops:
  0.6 185.7 %layer.1 = (bf16[176,1024]{1,0:T(8,128)(2,1)}, bf16[176,1024]{1,0:T(8,128)(2,1)}, bf16[176,1024]{1,0:T(8,128)(2,1)}, bf16[256,1024]{1,0:T(8,128)(2,1)}, bf16[128...) custom-call(s32[1,6]{1,0:T(1,128)} %lengths_ref.1, ...), custom_call_target="tpu_custom_call" | custom-call | tf_op jit(solution)/shard_map/layer/pallas_call | solution.py:1220
  186.4 6.3 %widen.1 = (bf16[176,1024]{1,0:T(8,128)(2,1)}, bf16[176,1024]{1,0:T(8,128)(2,1)}, bf16[176,1024]{1,0:T(8,128)(2,1)}, f32[256,1024]{1,0:T(8,128)}, f32[128,3072]{...) custom-call(bf16[176,1024]{1,0:T(8,128)(2,1)} %get-tuple-element.33., ...), custom_call_target="tpu_custom_call" | custom-call | tf_op jit(solution)/shard_map/widen/pallas_call | solution.py:1255
